TPU v7x, 32 devices: a whole 2x2x4 slice. The times are simulated.
32 devices in a mesh: grp: 2 (over y), fsdp: 8 (over z, x), seq: 2 (over core).
Axes of the slice: x: 2, y: 2, z: 4, core: 2. Of those that a mesh axis runs over, the one named last changes fastest.
Arguments:
- image_tokens: bfloat16 [16, 512, 3072], P(('grp', 'fsdp'), 'seq'), parts along dimension 0, may hold values from -6 to 6
- adjoint: bfloat16 [16, 512, 3072], P(('grp', 'fsdp'), 'seq'), parts along dimension 0, may hold values from -24 to 24
- attn_keys: bfloat16 [16, 768, 1536], P(('grp', 'fsdp'), 'seq'), parts along dimension 0, may hold values from -2.5 to 2.5
- attn_values: bfloat16 [16, 768, 1536], P(('grp', 'fsdp'), 'seq'), parts along dimension 0, may hold values from -6 to 6
- w_query: bfloat16 [3072, 1536], P('fsdp', 'seq'), may hold values from -0.109375 to 0.109375
- w_out: bfloat16 [1536, 3072], P('seq', 'fsdp'), may hold values from -0.15625 to 0.15625
- q_gain: float32 [128], replicated, may hold values from 1 to 2.5
- mod_table: float32 [28, 3, 3072], replicated, may hold values from -4 to 4
- timesteps: int32 [16], P(('grp', 'fsdp')), parts along dimension 0, may hold values from 0 to 27
- text_counts: int32 [16], P(('grp', 'fsdp')), parts along dimension 0, may hold values from 1 to 256
Outputs:
- branch_cotangent: float32 [16, 512, 3072], P(('grp', 'fsdp'), 'seq'), parts along dimension 0
There are 2 independent parts, one for each index of `grp`. A program takes and returns all parts, laid end to end along the dimension named above; an argument that names none is the same for every part. Nothing has to cross between parts.
Inputs may be any that keep to these rules, and one draw needn't show every extreme that they name: Of a prompt's 256 text keys, the first text_counts of them are real and the rest are padding.
All inputs are finite; a program needn't handle non-finite values.
Results may differ from a plain program's by a relative error of at most 0.0092.
Values may be sent and summed in bfloat16 or wider, within the bound.
A program may use at most 128 MiB of HBM per device.

v0:
```python
import jax
import jax.numpy as jnp
from jax import lax
from jax.sharding import PartitionSpec as P

HD = 128
SWAP = ((0, 1), (1, 0))


def contract_last(left, right):
    return lax.dot_general(
        left, right, (((1,), (1,)), ((), ())), preferred_element_type=jnp.float32
    )


def swap(piece):
    return lax.ppermute(piece, "seq", SWAP)


def local(
    image_tokens,
    adjoint,
    attn_keys,
    attn_values,
    w_query,
    w_out,
    q_gain,
    mod_table,
    timesteps,
    text_counts,
):
    me = lax.axis_index("seq")
    half = w_query.shape[1]
    heads = half // HD
    factor = HD ** (-0.5)
    w_q = lax.all_gather(w_query, "fsdp", axis=0, tiled=True)
    w_o = lax.all_gather(w_out.T, "fsdp", axis=0, tiled=True)
    modulation = lax.dynamic_index_in_dim(mod_table, timesteps[0], 0, keepdims=False)
    shift_row, scale_row, gate_row = (modulation[0], modulation[1], modulation[2])
    tokens = image_tokens[0].astype(jnp.float32)
    mean = jnp.mean(tokens, axis=-1, keepdims=True)
    centred = tokens - mean
    inv = lax.rsqrt(jnp.mean(centred * centred, axis=-1, keepdims=True) + 1e-06)
    normed = (centred * inv * (1.0 + scale_row) + shift_row).astype(jnp.bfloat16)
    d_branch = (gate_row * adjoint[0].astype(jnp.float32)).astype(jnp.bfloat16)

    def halves(rows):
        own = lax.dynamic_slice_in_dim(rows, me * half, half, 1)
        other = lax.dynamic_slice_in_dim(rows, (1 - me) * half, half, 1)
        return jnp.concatenate([own, swap(other)], axis=0)

    keys, values = (halves(attn_keys[0]), halves(attn_values[0]))
    key_rows = attn_keys.shape[1]
    txt = keys.shape[0] // 3
    spots = jnp.arange(key_rows, dtype=jnp.int32)
    positions = jnp.concatenate([me * key_rows + spots, (1 - me) * key_rows + spots])
    usable = (positions >= txt) | (positions < text_counts[0])
    normed_all = jnp.concatenate([normed, swap(normed)], axis=0)
    d_branch_all = jnp.concatenate([d_branch, swap(d_branch)], axis=0)
    query = jnp.dot(normed_all, w_q, preferred_element_type=jnp.float32)
    d_attn = jnp.dot(d_branch_all, w_o, preferred_element_type=jnp.float32).astype(jnp.bfloat16)
    parts = []
    for head in range(heads):
        cols = slice(head * HD, (head + 1) * HD)
        q_head, k_head, v_head = (query[:, cols], keys[:, cols], values[:, cols])
        root = lax.rsqrt(jnp.mean(q_head * q_head, axis=-1, keepdims=True) + 1e-06)
        unit = q_head * root
        q_normed = (unit * q_gain).astype(jnp.bfloat16)
        scores = contract_last(q_normed, k_head) * factor
        terms = jnp.where(usable[None, :], jnp.exp(scores), 0.0)
        probs = terms / jnp.sum(terms, axis=-1, keepdims=True)
        d_probs = contract_last(d_attn[:, cols], v_head)
        centre = jnp.sum(probs * d_probs, axis=-1, keepdims=True)
        d_scores = (probs * (d_probs - centre) * factor).astype(jnp.bfloat16)
        d_unit = jnp.dot(d_scores, k_head, preferred_element_type=jnp.float32) * q_gain
        d_query = root * (d_unit - unit * jnp.mean(d_unit * unit, axis=-1, keepdims=True))
        parts.append(d_query.astype(jnp.bfloat16))
    d_query = jnp.concatenate(parts, axis=1)
    count = tokens.shape[0]
    theirs = contract_last(d_query[count:], w_q).astype(jnp.bfloat16)
    mine = contract_last(d_query[:count], w_q)
    d_normed = mine + swap(theirs).astype(jnp.float32)
    d_hat = d_normed * (1.0 + scale_row)
    hat = centred * inv
    d_mean = jnp.mean(d_hat, axis=-1, keepdims=True)
    d_proj = jnp.mean(d_hat * hat, axis=-1, keepdims=True)
    return (inv * (d_hat - d_mean - hat * d_proj))[None]


def solution(mesh):
    in_specs = (
        P(("grp", "fsdp"), "seq", None),
        P(("grp", "fsdp"), "seq", None),
        P(("grp", "fsdp"), "seq", None),
        P(("grp", "fsdp"), "seq", None),
        P("fsdp", "seq"),
        P("seq", "fsdp"),
        P(),
        P(),
        P(("grp", "fsdp")),
        P(("grp", "fsdp")),
    )
    out_specs = P(("grp", "fsdp"), "seq", None)
    return jax.shard_map(local, mesh=mesh, in_specs=in_specs, out_specs=out_specs, check_vma=False)
```

profile of v0, /device:TPU:0, one launch (start us, length us, event | category | flops | bytes accessed | tf_op | source)
XLA Modules:
  0.0 214.6 jit_solution(10942834821170242803)
XLA Ops:
  6.5 0.7 all-gather.3.cloned.1.call-update
  7.3 0.0 all-gather.5.cloned.1.call-start
  7.3 0.7 all-gather.5.cloned.1.call-update
  8.7 1.7 convert_reduce_fusion
  10.4 0.6 fusion.12
  11.0 1.0 constant_dynamic-slice_fusion
  12.0 0.0 copy-start.9
  12.0 1.9 fusion.7
  13.9 0.5 collective-permute-start
  14.4 0.9 dynamic-slice_bitcast_fusion.2
  15.3 0.1 collective-permute-start.1
  15.3 0.5 copy-done.10
  15.9 0.9 dynamic-slice_bitcast_fusion
  16.8 0.1 collective-permute-start.3
  16.8 1.5 fusion.21
  18.3 0.5 collective-permute-start.2
  19.4 0.0 collective-permute-done.1
  19.5 0.0 collective-permute-done
  19.5 72.7 %all-gather.3.cloned.1.call-done = bf16[3072,768]{1,0:T(8,128)(2,1)} async-done(((bf16[384,768]{1,0:T(8,128)(2,1)}), bf16[3072,768]{1,0:T(8,128)(2,1)}) %all-gather.3.cloned.1.call-update) | async-done | bytes 4718608 | tf_op jit(solution)/shard_map/all_gather | solution.py:36
  92.2 5.9 %fusion.13 = f32[512,768]{1,0:T(8,128)S(1)} fusion(bf16[3072,768]{1,0:T(8,128)(2,1)} %all-gather.3.cloned.1.call-done, bf16[256,3072]{1,0:T(8,128)(2,1)} %collective-permute-done, bf16[256,3072]{1,0:T(8,128)(2,1)} %fusion.7), kind=kOutput, calls=%fused_computation.16 | convolution fusion | flops 2422210560 | bytes 9437184 | tf_op jit(solution)/shard_map/dot_general | solution.py:60
  98.1 0.0 copy-start.23
  98.1 0.5 multiply_reduce_fusion.7
  98.6 0.1 copy-done.23
  98.7 2.2 %fusion.116 = (f32[512]{0:T(512)}, f32[512,768]{1,0:T(8,128)}) fusion(bf16[384,768]{1,0:T(8,128)(2,1)S(1)} %get-tuple-element.20, bf16[384,768]{1,0:T(8,128)(2,1)S(1)} %collective-permute-done.1, f32[512,768]{1,0:T(8,128)S(1)} %fusion.13, f32[512]{0:T(512)S(1)} %get-tuple-element.56, f32[128]{0:T(128)S(1)} %copy-done.23, pred[768]{0:T(1024)(128)(4,1)S(1)} %compare_or_fusion), kind=kOutput, calls=%fused_computation.213 | convolution fusion | flops 102432256 | bytes 3020288 | tf_op jit(solution)/shard_map/dot_general | solution.py:11
  101.0 2.2 %fusion.111 = (f32[512]{0:T(512)}, f32[512,768]{1,0:T(8,128)}) fusion(bf16[384,768]{1,0:T(8,128)(2,1)S(1)} %get-tuple-element.20, bf16[384,768]{1,0:T(8,128)(2,1)S(1)} %collective-permute-done.1, f32[512,768]{1,0:T(8,128)S(1)} %fusion.13, f32[128]{0:T(128)S(1)} %copy-done.23, f32[512]{0:T(512)S(1)} %get-tuple-element.57, pred[768]{0:T(1024)(128)(4,1)S(1)} %compare_or_fusion), kind=kOutput, calls=%fused_computation.208 | convolution fusion | flops 102432256 | bytes 3020288 | tf_op jit(solution)/shard_map/dot_general | solution.py:11
  103.2 2.3 %fusion.114 = (f32[512]{0:T(512)}, f32[512,768]{1,0:T(8,128)}) fusion(bf16[384,768]{1,0:T(8,128)(2,1)S(1)} %get-tuple-element.20, bf16[384,768]{1,0:T(8,128)(2,1)S(1)} %collective-permute-done.1, f32[512,768]{1,0:T(8,128)S(1)} %fusion.13, f32[512]{0:T(512)S(1)} %get-tuple-element.54, f32[128]{0:T(128)S(1)} %copy-done.23, pred[768]{0:T(1024)(128)(4,1)S(1)} %compare_or_fusion), kind=kOutput, calls=%fused_computation.211 | convolution fusion | flops 102432256 | bytes 3020288 | tf_op jit(solution)/shard_map/dot_general | solution.py:11
  105.5 2.2 %fusion.115 = (f32[512]{0:T(512)}, f32[512,768]{1,0:T(8,128)}) fusion(bf16[384,768]{1,0:T(8,128)(2,1)S(1)} %get-tuple-element.20, bf16[384,768]{1,0:T(8,128)(2,1)S(1)} %collective-permute-done.1, f32[512,768]{1,0:T(8,128)S(1)} %fusion.13, f32[512]{0:T(512)S(1)} %get-tuple-element.55, f32[128]{0:T(128)S(1)} %copy-done.23, pred[768]{0:T(1024)(128)(4,1)S(1)} %compare_or_fusion), kind=kOutput, calls=%fused_computation.212 | convolution fusion | flops 102432256 | bytes 3020288 | tf_op jit(solution)/shard_map/dot_general | solution.py:11
  107.7 2.2 %fusion.113 = (f32[512]{0:T(512)}, f32[512,768]{1,0:T(8,128)}) fusion(bf16[384,768]{1,0:T(8,128)(2,1)S(1)} %get-tuple-element.20, bf16[384,768]{1,0:T(8,128)(2,1)S(1)} %collective-permute-done.1, f32[512,768]{1,0:T(8,128)S(1)} %fusion.13, f32[512]{0:T(512)S(1)} %get-tuple-element.53, f32[128]{0:T(128)S(1)} %copy-done.23, pred[768]{0:T(1024)(128)(4,1)S(1)} %compare_or_fusion), kind=kOutput, calls=%fused_computation.210 | convolution fusion | flops 102432256 | bytes 3020288 | tf_op jit(solution)/shard_map/dot_general | solution.py:11
  109.9 2.2 %fusion.112 = (f32[512]{0:T(512)}, f32[512,768]{1,0:T(8,128)}) fusion(bf16[768,128]{1,0:T(8,128)(2,1)S(1)} %pad_maximum_fusion.2, f32[512,768]{1,0:T(8,128)S(1)} %fusion.13, f32[512]{0:T(512)S(1)} %get-tuple-element.52, f32[128]{0:T(128)S(1)} %copy-done.23, pred[768]{0:T(1024)(128)(4,1)S(1)} %compare_or_fusion), kind=kOutput, calls=%fused_computation.209 | convolution fusion | flops 102039040 | bytes 2037248 | tf_op jit(solution)/shard_map/dot_general | solution.py:11
  112.1 0.0 collective-permute-done.2
  112.1 61.2 %all-gather.5.cloned.1.call-done = bf16[3072,768]{0,1:T(8,128)(2,1)} async-done(((bf16[384,768]{0,1:T(8,128)(2,1)}), bf16[3072,768]{0,1:T(8,128)(2,1)}) %all-gather.5.cloned.1.call-update) | async-done | bytes 4718608 | tf_op jit(solution)/shard_map/all_gather | solution.py:37
  173.4 6.0 %fusion.22 = bf16[512,768]{1,0:T(8,128)(2,1)S(1)} fusion(bf16[3072,768]{0,1:T(8,128)(2,1)} %all-gather.5.cloned.1.call-done, bf16[256,3072]{1,0:T(8,128)(2,1)} %collective-permute-done.2, bf16[256,3072]{1,0:T(8,128)(2,1)} %fusion.21), kind=kOutput, calls=%fused_computation.65 | convolution fusion | flops 2422603776 | bytes 8650752 | tf_op jit(solution)/shard_map/dot_general | solution.py:61
  179.4 0.0 collective-permute-done.3
  179.5 0.0 copy-start.24
  179.5 1.4 multiply_reduce_fusion.4
  180.9 0.0 copy-start.8
  180.9 0.5 convolution_multiply_fusion.4
  181.4 0.9 copy-done.8
  182.3 1.4 multiply_reduce_fusion.5
  183.7 0.5 convolution_multiply_fusion.5
  184.2 0.9 copy-done.6
  185.1 1.4 multiply_reduce_fusion.2
  186.5 0.7 convolution_multiply_fusion.2
  187.1 0.7 copy-done.5
  187.9 1.4 multiply_reduce_fusion.3
  189.2 0.5 convolution_multiply_fusion.3
  189.7 0.9 copy-done.4
  190.6 1.5 multiply_reduce_fusion.1
  192.1 1.4 multiply_reduce_fusion
  193.6 0.5 convolution_multiply_fusion.1
  194.1 0.8 copy-done.2
  195.0 0.0 slice-start.1
  195.0 1.2 multiply_reduce_fusion.6
  196.2 0.2 fusion.63
  196.4 0.3 fusion.64
  196.7 0.3 fusion.65
  196.9 0.3 fusion.66
  197.2 0.3 fusion.67
  197.4 0.3 fusion.68
  197.8 1.4 convolution_convert_fusion
  199.2 0.1 collective-permute-start.4
  199.3 3.4 %collective-permute-done.4 = bf16[256,3072]{1,0:T(8,128)(2,1)S(1)} collective-permute-done((bf16[256,3072]{1,0:T(8,128)(2,1)S(1)}, bf16[256,3072]{1,0:T(8,128)(2,1)S(1)}, u32[]{:S(2)}, u32[]{:S(2)}) %collective-permute-start.4) | collective-permute-done | bytes 1572896 | tf_op jit(solution)/shard_map/ppermute | solution.py:17
  202.7 2.0 fusion.25
  204.7 3.0 %fusion.11 = f32[1,256,3072]{2,1,0:T(8,128)} fusion(bf16[1,256,3072]{2,1,0:T(8,128)(2,1)S(1)} %copy-done, f32[256]{0:T(256)S(1)} %broadcast_multiply_fusion.6, f32[256]{0:T(256)S(1)} %broadcast_multiply_fusion.7, f32[256]{0:T(256)S(1)} %copy-done.26, f32[256]{0:T(256)S(1)} %copy-done.22, f32[3072]{0:T(1024)S(1)} %bitcast.60, ...), kind=kLoop, calls=%fused_computation.14 | loop fusion | flops 7864320 | bytes 9453568 | tf_op jit(solution)/shard_map/broadcast_in_dim | solution.py:87
  (82 shorter events, 0.2 us)
Async XLA Ops:
  6.5 3.8 %copy-start = (bf16[1,256,3072]{2,1,0:T(8,128)(2,1)S(1)}, bf16[1,256,3072]{2,1,0:T(8,128)(2,1)}, u32[]{:S(2)}) copy-start(bf16[1,256,3072]{2,1,0:T(8,128)(2,1)} %param.10) | copy-start | bytes 4718596
  6.5 85.6 %all-gather.3.cloned.1.call-start = ((), (), s32[]{:S(2)}) async-start(), calls=%async_computation | async-start | bytes 5308416 | tf_op jit(solution)/shard_map/all_gather | solution.py:36
  7.3 166.1 %all-gather.5.cloned.1.call-start = ((), (), s32[]{:S(2)}) async-start(), calls=%async_computation.1 | async-start | bytes 5308416 | tf_op jit(solution)/shard_map/all_gather | solution.py:37
  10.4 3.6 %copy-start.21 = (f32[256]{0:T(256)}, f32[256]{0:T(256)S(1)}, u32[]{:S(2)}) copy-start(f32[256]{0:T(256)S(1)} %broadcast_multiply_fusion.8) | copy-start | bytes 3076
  10.9 3.0 %copy-start.25 = (f32[256]{0:T(256)}, f32[256]{0:T(256)S(1)}, u32[]{:S(2)}) copy-start(f32[256]{0:T(256)S(1)} %add_rsqrt_fusion.6) | copy-start | bytes 3076
  12.0 2.4 %copy-start.9 = (bf16[1,384,1536]{2,1,0:T(8,128)(2,1)S(1)}, bf16[1,384,1536]{2,1,0:T(8,128)(2,1)}, u32[]{:S(2)}) copy-start(bf16[1,384,1536]{2,1,0:T(8,128)(2,1)} %param.12) | copy-start | bytes 3538948
  13.9 5.5 %collective-permute-start = (bf16[256,3072]{1,0:T(8,128)(2,1)}, bf16[256,3072]{1,0:T(8,128)(2,1)}, u32[]{:S(2)}, u32[]{:S(2)}) collective-permute-start(bf16[256,3072]{1,0:T(8,128)(2,1)} %fusion.7), channel_id=1, source_target_pairs={{0,1},{1,0},{2,3},{3,2},{4,5},{5,4},{6,7},{7,6},{8,9},{9,8},{10,11... | collective-permute-start | bytes 4718600 | tf_op jit(solution)/shard_map/ppermute | solution.py:17
  14.4 1.5 copy-start.10
  15.3 1.6 copy-start.3
  15.3 4.2 %collective-permute-start.1 = (bf16[384,768]{1,0:T(8,128)(2,1)}, bf16[384,768]{1,0:T(8,128)(2,1)S(1)}, u32[]{:S(2)}, u32[]{:S(2)}) collective-permute-start(bf16[384,768]{1,0:T(8,128)(2,1)} %get-tuple-element.19), channel_id=1, source_target_pairs={{0,1},{1,0},{2,3},{3,2},{4,5},{5,4},{6,7},{7,6},{8,9},{9,8},{10,11... | collective-permute-start | bytes 1769480 | tf_op jit(solution)/shard_map/ppermute | solution.py:17
  16.8 162.7 %collective-permute-start.3 = (bf16[384,768]{1,0:T(8,128)(2,1)}, bf16[384,768]{1,0:T(8,128)(2,1)}, u32[]{:S(2)}, u32[]{:S(2)}) collective-permute-start(bf16[384,768]{1,0:T(8,128)(2,1)} %get-tuple-element.24), channel_id=1, source_target_pairs={{0,1},{1,0},{2,3},{3,2},{4,5},{5,4},{6,7},{7,6},{8,9},{9,8},{10,11... | collective-permute-start | bytes 1769480 | tf_op jit(solution)/shard_map/ppermute | solution.py:17
  18.3 93.9 %collective-permute-start.2 = (bf16[256,3072]{1,0:T(8,128)(2,1)}, bf16[256,3072]{1,0:T(8,128)(2,1)}, u32[]{:S(2)}, u32[]{:S(2)}) collective-permute-start(bf16[256,3072]{1,0:T(8,128)(2,1)} %fusion.21), channel_id=1, source_target_pairs={{0,1},{1,0},{2,3},{3,2},{4,5},{5,4},{6,7},{7,6},{8,9},{9,8},{10,11... | collective-permute-start | bytes 4718600 | tf_op jit(solution)/shard_map/ppermute | solution.py:17
  98.1 11.8 %copy-start.1 = (f32[512,768]{1,0:T(8,128)}, f32[512,768]{1,0:T(8,128)S(1)}, u32[]{:S(2)}) copy-start(f32[512,768]{1,0:T(8,128)S(1)} %fusion.13) | copy-start | bytes 4718596
  98.1 0.7 copy-start.23
  98.6 9.1 %copy-start.11 = (f32[512]{0:T(512)}, f32[512]{0:T(512)S(1)}, u32[]{:S(2)}) copy-start(f32[512]{0:T(512)S(1)} %get-tuple-element.53) | copy-start | bytes 6148
  98.6 11.3 %copy-start.27 = (f32[512]{0:T(512)}, f32[512]{0:T(512)S(1)}, u32[]{:S(2)}) copy-start(f32[512]{0:T(512)S(1)} %get-tuple-element.52) | copy-start | bytes 6148
  98.6 2.3 %copy-start.15 = (f32[512]{0:T(512)}, f32[512]{0:T(512)S(1)}, u32[]{:S(2)}) copy-start(f32[512]{0:T(512)S(1)} %get-tuple-element.56) | copy-start | bytes 6148
  98.6 4.6 %copy-start.17 = (f32[512]{0:T(512)}, f32[512]{0:T(512)S(1)}, u32[]{:S(2)}) copy-start(f32[512]{0:T(512)S(1)} %get-tuple-element.57) | copy-start | bytes 6148
  101.0 4.5 %copy-start.13 = (f32[512]{0:T(512)}, f32[512]{0:T(512)S(1)}, u32[]{:S(2)}) copy-start(f32[512]{0:T(512)S(1)} %get-tuple-element.54) | copy-start | bytes 6148
  101.0 4.5 %copy-start.19 = (f32[512]{0:T(512)}, f32[512]{0:T(512)S(1)}, u32[]{:S(2)}) copy-start(f32[512]{0:T(512)S(1)} %get-tuple-element.55) | copy-start | bytes 6148
  112.1 67.3 %copy-start.32 = (f32[512]{0:T(512)S(1)}, f32[512]{0:T(512)}, u32[]{:S(2)}) copy-start(f32[512]{0:T(512)} %get-tuple-element.46) | copy-start | bytes 6148
  173.4 6.1 %copy-start.7 = (f32[512,768]{1,0:T(8,128)S(1)}, f32[512,768]{1,0:T(8,128)}, u32[]{:S(2)}) copy-start(f32[512,768]{1,0:T(8,128)} %get-tuple-element.47) | copy-start | bytes 4718596
  179.5 1.4 copy-start.24
  180.9 1.4 copy-start.8
  180.9 1.4 copy-start.33
  183.7 1.4 copy-start.6
  183.7 1.4 copy-start.31
  186.4 1.4 copy-start.5
  186.4 1.4 copy-start.30
  189.2 1.4 copy-start.4
  189.2 1.4 copy-start.29
  190.6 1.5 copy-start.34
  190.6 1.5 copy-start.35
  193.5 1.4 copy-start.2
  193.5 1.4 copy-start.12
  193.5 1.4 copy-start.14
  193.5 1.4 copy-start.16
  193.5 1.4 copy-start.18
  193.6 1.4 copy-start.20
  193.6 1.4 copy-start.28
  193.6 4.1 %slice-start = ((s8[4718592]{0:T(1024)(128)(4,1)}), s8[4194304]{0:T(1024)(128)(4,1)S(1)}, s32[]{:S(2)}) async-start(s8[4718592]{0:T(1024)(128)(4,1)} %bitcast.63), calls=%async_computation.2 | async-start | bytes 8388608
  195.0 2.8 %slice-start.1 = ((s8[4718592]{0:T(1024)(128)(4,1)}), s8[524288]{0:T(1024)(128)(4,1)S(1)}, s32[]{:S(2)}) async-start(s8[4718592]{0:T(1024)(128)(4,1)} %bitcast.63), calls=%async_computation.3 | async-start | bytes 1048576
  197.7 4.9 %copy-start.22 = (f32[256]{0:T(256)S(1)}, f32[256]{0:T(256)}, u32[]{:S(2)}) copy-start(f32[256]{0:T(256)} %copy-done.21) | copy-start | bytes 3076
  197.7 4.9 %copy-start.26 = (f32[256]{0:T(256)S(1)}, f32[256]{0:T(256)}, u32[]{:S(2)}) copy-start(f32[256]{0:T(256)} %copy-done.25) | copy-start | bytes 3076
  199.2 3.5 %collective-permute-start.4 = (bf16[256,3072]{1,0:T(8,128)(2,1)S(1)}, bf16[256,3072]{1,0:T(8,128)(2,1)S(1)}, u32[]{:S(2)}, u32[]{:S(2)}) collective-permute-start(bf16[256,3072]{1,0:T(8,128)(2,1)S(1)} %convolution_convert_fusion), channel_id=1, source_target_pairs={{0,1},{1,0},{2,3},{3,2},{4,5},{5,4},{6,7},{7,6},{8,9},{9,8},{10,11... | collective-permute-start | bytes 4718600 | tf_op jit(solution)/shard_map/ppermute | solution.py:17
Sparse Core Ops, SparseCore 0:
  9.5 82.5 all-gather.2
  94.2 79.1 all-gather.4
where the time goes:
time: 215 us
  waiting for transfers between devices  139 us (65%)
  matrix products  40.9 us (19%)
  between operations  15.3 us (7%)
  other arithmetic  11.8 us (5%)
  local copies, waits for them, and re-layouts  6.78 us (3%)
    all_gather x1, waiting for transfers between devices, local(): w_q = lax.all_gather(w_query, 'fsdp', axis=0, tiled=True)  72.7 us
    all_gather x1, waiting for transfers between devices, local(): w_o = lax.all_gather(w_out.T, 'fsdp', axis=0, tiled=True)  61.2 us
    dot_general x14, matrix products, contract_last(): lax.dot_general(left, right, (((1,), (1,)), ((), ())), preferred_element_...  25.1 us
    dot_general x1, matrix products, local(): jnp.dot(d_branch_all, w_o, preferred_element_type=jnp.float32)  6.04 us
    dot_general x1, matrix products, local(): query = jnp.dot(normed_all, w_q, preferred_element_type=jnp.float32)  5.89 us
    unnamed x76, local copies, waits for them, and re-layouts  5.01 us
  transfers between devices with their start and end apart: 7, of which 3 were waited for; matrix products, arithmetic and copies ran while one was open for 16% of the time, Pallas kernels for 0%

commit v1 on v0

--- a/solution.py
+++ b/solution.py
@@ -33,7 +33,12 @@
     half = w_query.shape[1]
     heads = half // HD
     factor = HD ** (-0.5)
-    w_q = lax.all_gather(w_query, "fsdp", axis=0, tiled=True)
+    ring = [w_query]
+    for hop in range(7):
+        ring.append(lax.ppermute(ring[-1], "fsdp", [(dev, (dev + 1) % 8) for dev in range(8)]))
+    w_q = jnp.roll(
+        jnp.concatenate(ring[::-1], axis=0), (lax.axis_index("fsdp") + 1) * ring[0].shape[0], axis=0
+    )
     w_o = lax.all_gather(w_out.T, "fsdp", axis=0, tiled=True)
     modulation = lax.dynamic_index_in_dim(mod_table, timesteps[0], 0, keepdims=False)
     shift_row, scale_row, gate_row = (modulation[0], modulation[1], modulation[2])

time: 215 us -> 230 us (1.070)
  local copies, waits for them, and re-layouts: 6.78 us -> 19.3 us
  starting transfers between devices: 1.13 us -> 3.52 us
    ppermute x0 -> x7, waiting for transfers between devices: none -> 135 us  [local(): lax.ppermute(ring[-1], 'fsdp', [(dev, (dev + 1) % 8) for dev in range(8)])]
    all_gather x1 -> x0, waiting for transfers between devices: 72.7 us -> none  [local(): w_q = lax.all_gather(w_query, 'fsdp', axis=0, tiled=True)]
    all_gather x1, waiting for transfers between devices: 61.2 us -> 0.01 us  [local(): w_o = lax.all_gather(w_out.T, 'fsdp', axis=0, tiled=True)]
    unnamed x76 -> x97, local copies, waits for them, and re-layouts: 5.01 us -> 16 us
    ppermute x0 -> x7, starting transfers between devices: none -> 2.95 us  [local(): lax.ppermute(ring[-1], 'fsdp', [(dev, (dev + 1) % 8) for dev in range(8)])]
  transfers between devices with their start and end apart: 7 -> 13, of which waited for: 3 -> 8; matrix products, arithmetic and copies ran while one was open for 16% -> 20% of each run, Pallas kernels for 0% -> 0%
where the time goes in v1:
time: 230 us; the launch traced here: 229 us
  waiting for transfers between devices  138 us (60%)
  matrix products  42.3 us (18%)
  local copies, waits for them, and re-layouts  19.3 us (8%)
  between operations  15.4 us (7%)
  other arithmetic  10.1 us (4%)
  starting transfers between devices  3.52 us (2%)
    ppermute x7, waiting for transfers between devices, local(): lax.ppermute(ring[-1], 'fsdp', [(dev, (dev + 1) % 8) for dev in range(8)])  135 us
    dot_general x14, matrix products, contract_last(): lax.dot_general(left, right, (((1,), (1,)), ((), ())), preferred_element_...  25.6 us
    unnamed x97, local copies, waits for them, and re-layouts  16 us
    dot_general x1, matrix products, local(): query = jnp.dot(normed_all, w_q, preferred_element_type=jnp.float32)  6.94 us
    dot_general x1, matrix products, local(): jnp.dot(d_branch_all, w_o, preferred_element_type=jnp.float32)  6.07 us
  transfers between devices with their start and end apart: 13, of which 8 were waited for; matrix products, arithmetic and copies ran while one was open for 20% of the time, Pallas kernels for 0%

profile of v1, /device:TPU:0, one launch (start us, length us, event | category | flops | bytes accessed | tf_op | source)
XLA Modules:
  0.0 228.9 jit_solution(4010455965681873788)
XLA Ops:
  6.5 2.9 %collective-permute-start.1 = (bf16[384,768]{1,0:T(8,128)(2,1)}, bf16[384,768]{1,0:T(8,128)(2,1)S(1)}, u32[]{:S(2)}, u32[]{:S(2)}) collective-permute-start(bf16[384,768]{1,0:T(8,128)(2,1)} %param.14), channel_id=1, source_target_pairs={{0,2},{2,4},{4,6},{6,8},{8,10},{10,12},{12,14},{14,0},{1,3},{3,5},... | collective-permute-start | bytes 1769480 | tf_op jit(solution)/shard_map/ppermute | solution.py:38
  9.5 16.6 %collective-permute-done.1 = bf16[384,768]{1,0:T(8,128)(2,1)S(1)} collective-permute-done((bf16[384,768]{1,0:T(8,128)(2,1)}, bf16[384,768]{1,0:T(8,128)(2,1)S(1)}, u32[]{:S(2)}, u32[]{:S(2)}) %collective-permute-start.1) | collective-permute-done | bytes 589856 | tf_op jit(solution)/shard_map/ppermute | solution.py:38
  26.1 17.2 %collective-permute-done.2 = bf16[384,768]{1,0:T(8,128)(2,1)S(1)} collective-permute-done((bf16[384,768]{1,0:T(8,128)(2,1)S(1)}, bf16[384,768]{1,0:T(8,128)(2,1)S(1)}, u32[]{:S(2)}, u32[]{:S(2)}) %collective-permute-start.2) | collective-permute-done | bytes 589856 | tf_op jit(solution)/shard_map/ppermute | solution.py:38
  43.3 16.4 %collective-permute-done.3 = bf16[384,768]{1,0:T(8,128)(2,1)} collective-permute-done((bf16[384,768]{1,0:T(8,128)(2,1)S(1)}, bf16[384,768]{1,0:T(8,128)(2,1)}, u32[]{:S(2)}, u32[]{:S(2)}) %collective-permute-start.3) | collective-permute-done | bytes 589856 | tf_op jit(solution)/shard_map/ppermute | solution.py:38
  59.7 2.1 dynamic-slice_bitcast_fusion.2
  61.8 0.3 convert_reduce_fusion
  62.2 14.2 %collective-permute-done.4 = bf16[384,768]{1,0:T(8,128)(2,1)} collective-permute-done((bf16[384,768]{1,0:T(8,128)(2,1)}, bf16[384,768]{1,0:T(8,128)(2,1)}, u32[]{:S(2)}, u32[]{:S(2)}) %collective-permute-start.4) | collective-permute-done | bytes 589856 | tf_op jit(solution)/shard_map/ppermute | solution.py:38
  76.4 0.6 fusion.17
  77.6 1.0 dynamic-slice_add_fusion
  78.7 24.4 %collective-permute-done.5 = bf16[384,768]{1,0:T(8,128)(2,1)} collective-permute-done((bf16[384,768]{1,0:T(8,128)(2,1)}, bf16[384,768]{1,0:T(8,128)(2,1)}, u32[]{:S(2)}, u32[]{:S(2)}) %collective-permute-start.5) | collective-permute-done | bytes 589856 | tf_op jit(solution)/shard_map/ppermute | solution.py:38
  103.1 1.9 fusion.12
  105.0 1.1 dynamic-slice_bitcast_fusion
  106.2 0.5 collective-permute-start.10
  106.6 19.4 %collective-permute-done.6 = bf16[384,768]{1,0:T(8,128)(2,1)} collective-permute-done((bf16[384,768]{1,0:T(8,128)(2,1)}, bf16[384,768]{1,0:T(8,128)(2,1)}, u32[]{:S(2)}, u32[]{:S(2)}) %collective-permute-start.6) | collective-permute-done | bytes 589856 | tf_op jit(solution)/shard_map/ppermute | solution.py:38
  126.0 1.5 fusion.25
  128.2 26.6 %collective-permute-done.7 = bf16[384,768]{1,0:T(8,128)(2,1)} collective-permute-done((bf16[384,768]{1,0:T(8,128)(2,1)}, bf16[384,768]{1,0:T(8,128)(2,1)}, u32[]{:S(2)}, u32[]{:S(2)}) %collective-permute-start.7) | collective-permute-done | bytes 589856 | tf_op jit(solution)/shard_map/ppermute | solution.py:38
  154.8 1.1 constant_dynamic-update-slice_fusion.15
  155.9 1.1 constant_dynamic-update-slice_fusion.14
  157.1 1.2 constant_dynamic-update-slice_fusion.13
  158.2 1.1 constant_dynamic-update-slice_fusion.12
  159.4 1.2 constant_dynamic-update-slice_fusion.11
  160.7 1.1 constant_dynamic-update-slice_fusion.7
  161.8 1.1 constant_dynamic-update-slice_fusion.6
  162.9 1.1 constant_dynamic-update-slice_fusion.5
  164.0 1.1 constant_dynamic-update-slice_fusion.4
  165.1 1.1 constant_dynamic-update-slice_fusion.3
  166.4 6.9 %fusion.3 = f32[512,768]{1,0:T(8,128)S(1)} fusion(bf16[6144,768]{1,0:T(8,128)(2,1)S(1)} %constant_dynamic-update-slice_fusion, s32[]{:T(128)S(6)} %select_n.46, bf16[256,3072]{1,0:T(8,128)(2,1)} %collective-permute-done, bf16[256,3072]{1,0:T(8,128)(2,1)} %fusion.12), kind=kOutput, calls=%fused_computation.7 | convolution fusion | flops 2422210560 | bytes 9437188 | tf_op jit(solution)/shard_map/dot_general | solution.py:65
  173.4 0.5 multiply_reduce_fusion.7
  173.9 0.1 copy-done.25
  174.1 2.2 fusion.117
  176.3 2.2 fusion.119
  178.5 2.2 fusion.120
  180.7 2.2 fusion.121
  182.9 2.2 fusion.122
  185.1 2.3 fusion.118
  187.4 6.1 %fusion.26 = bf16[512,768]{1,0:T(8,128)(2,1)S(1)} fusion(bf16[3072,768]{0,1:T(8,128)(2,1)} %all-gather.2.cloned.1.call-done, bf16[256,3072]{1,0:T(8,128)(2,1)} %collective-permute-done.9, bf16[256,3072]{1,0:T(8,128)(2,1)} %fusion.25), kind=kOutput, calls=%fused_computation.69 | convolution fusion | flops 2422603776 | bytes 8650752 | tf_op jit(solution)/shard_map/dot_general | solution.py:66
  193.5 1.4 multiply_reduce_fusion.5
  194.9 0.5 convolution_multiply_fusion.5
  195.5 0.9 copy-done.10
  196.3 1.4 multiply_reduce_fusion.1
  197.7 0.5 convolution_multiply_fusion.1
  198.2 0.9 copy-done.9
  199.1 1.4 multiply_reduce_fusion.2
  200.5 0.5 convolution_multiply_fusion.2
  200.9 0.9 copy-done.8
  201.9 1.4 multiply_reduce_fusion.3
  203.2 0.7 convolution_multiply_fusion.3
  203.9 0.7 copy-done.7
  204.6 1.4 multiply_reduce_fusion.4
  206.1 0.5 convolution_multiply_fusion.4
  206.5 0.9 copy-done.36
  207.4 1.5 multiply_reduce_fusion
  209.0 1.1 multiply_reduce_fusion.6
  210.1 0.2 fusion.65
  210.4 0.3 fusion.66
  210.7 0.3 fusion.67
  210.9 0.3 fusion.68
  211.2 0.3 fusion.69
  211.5 0.3 fusion.70
  211.8 1.4 convolution_convert_fusion
  213.3 0.1 collective-permute-start.11
  213.3 3.4 %collective-permute-done.11 = bf16[256,3072]{1,0:T(8,128)(2,1)S(1)} collective-permute-done((bf16[256,3072]{1,0:T(8,128)(2,1)S(1)}, bf16[256,3072]{1,0:T(8,128)(2,1)S(1)}, u32[]{:S(2)}, u32[]{:S(2)}) %collective-permute-start.11) | collective-permute-done | bytes 1572896 | tf_op jit(solution)/shard_map/ppermute | solution.py:17
  216.7 2.5 %fusion.116 = (f32[256]{0:T(256)S(1)}, f32[256]{0:T(256)S(1)}, f32[256,3072]{1,0:T(8,128)S(1)}) fusion(f32[256]{0:T(256)S(1)} %copy-done.28, f32[256]{0:T(256)S(1)} %copy-done.24, bf16[1,256,3072]{2,1,0:T(8,128)(2,1)S(1)} %copy-done, f32[3072]{0:T(1024)S(1)} %bitcast.56, bf16[256,3072]{1,0:T(8,128)(2,1)S(1)} %collective-permute-done.11, ...), kind=kOutput, calls=%fused_computation.229 | convolution fusion | flops 1215036928 | bytes 11419652 | tf_op jit(solution)/shard_map/dot_general | solution.py:11
  219.3 2.8 %fusion.16 = f32[1,256,3072]{2,1,0:T(8,128)} fusion(bf16[1,256,3072]{2,1,0:T(8,128)(2,1)S(1)} %copy-done, f32[256,3072]{1,0:T(8,128)S(1)} %get-tuple-element.51, f32[256]{0:T(256)S(1)} %broadcast_multiply_fusion.6, f32[256]{0:T(256)S(1)} %broadcast_multiply_fusion.7, f32[256]{0:T(256)S(1)} %copy-done.28, f32[256]{0:T(256)S(1)} %copy-done.24), kind=kLoop, calls=%fused_computation.20 | loop fusion | flops 5505024 | bytes 7868416 | tf_op jit(solution)/shard_map/broadcast_in_dim | solution.py:92
  (115 shorter events, 0.6 us)
Async XLA Ops:
  6.5 55.3 %copy-start = (bf16[1,256,3072]{2,1,0:T(8,128)(2,1)S(1)}, bf16[1,256,3072]{2,1,0:T(8,128)(2,1)}, u32[]{:S(2)}) copy-start(bf16[1,256,3072]{2,1,0:T(8,128)(2,1)} %param.10) | copy-start | bytes 4718596
  6.5 180.8 %all-gather.2.cloned.1.call-start = ((), (), s32[]{:S(2)}) async-start(), calls=%async_computation | async-start | bytes 5308416 | tf_op jit(solution)/shard_map/all_gather | solution.py:42
  6.5 19.5 %collective-permute-start.1 = (bf16[384,768]{1,0:T(8,128)(2,1)}, bf16[384,768]{1,0:T(8,128)(2,1)S(1)}, u32[]{:S(2)}, u32[]{:S(2)}) collective-permute-start(bf16[384,768]{1,0:T(8,128)(2,1)} %param.14), channel_id=1, source_target_pairs={{0,2},{2,4},{4,6},{6,8},{8,10},{10,12},{12,14},{14,0},{1,3},{3,5},... | collective-permute-start | bytes 1769480 | tf_op jit(solution)/shard_map/ppermute | solution.py:38
  26.1 17.2 %collective-permute-start.2 = (bf16[384,768]{1,0:T(8,128)(2,1)S(1)}, bf16[384,768]{1,0:T(8,128)(2,1)S(1)}, u32[]{:S(2)}, u32[]{:S(2)}) collective-permute-start(bf16[384,768]{1,0:T(8,128)(2,1)S(1)} %collective-permute-done.1), channel_id=1, source_target_pairs={{0,2},{2,4},{4,6},{6,8},{8,10},{10,12},{12,14},{14,0},{1,3},{3,5},... | collective-permute-start | bytes 1769480 | tf_op jit(solution)/shard_map/ppermute | solution.py:38
  43.3 18.6 %copy-start.4 = (bf16[384,768]{1,0:T(8,128)(2,1)}, bf16[384,768]{1,0:T(8,128)(2,1)S(1)}, u32[]{:S(2)}) copy-start(bf16[384,768]{1,0:T(8,128)(2,1)S(1)} %collective-permute-done.2) | copy-start | bytes 1769476
  43.3 16.4 %collective-permute-start.3 = (bf16[384,768]{1,0:T(8,128)(2,1)S(1)}, bf16[384,768]{1,0:T(8,128)(2,1)}, u32[]{:S(2)}, u32[]{:S(2)}) collective-permute-start(bf16[384,768]{1,0:T(8,128)(2,1)S(1)} %collective-permute-done.2), channel_id=1, source_target_pairs={{0,2},{2,4},{4,6},{6,8},{8,10},{10,12},{12,14},{14,0},{1,3},{3,5},... | collective-permute-start | bytes 1769480 | tf_op jit(solution)/shard_map/ppermute | solution.py:38
  59.7 16.7 %collective-permute-start.4 = (bf16[384,768]{1,0:T(8,128)(2,1)}, bf16[384,768]{1,0:T(8,128)(2,1)}, u32[]{:S(2)}, u32[]{:S(2)}) collective-permute-start(bf16[384,768]{1,0:T(8,128)(2,1)} %collective-permute-done.3), channel_id=1, source_target_pairs={{0,2},{2,4},{4,6},{6,8},{8,10},{10,12},{12,14},{14,0},{1,3},{3,5},... | collective-permute-start | bytes 1769480 | tf_op jit(solution)/shard_map/ppermute | solution.py:38
  61.8 66.3 %collective-permute-start.8 = (bf16[384,768]{1,0:T(8,128)(2,1)}, bf16[384,768]{1,0:T(8,128)(2,1)S(1)}, u32[]{:S(2)}, u32[]{:S(2)}) collective-permute-start(bf16[384,768]{1,0:T(8,128)(2,1)} %get-tuple-element.19), channel_id=1, source_target_pairs={{0,1},{1,0},{2,3},{3,2},{4,5},{5,4},{6,7},{7,6},{8,9},{9,8},{10,11... | collective-permute-start | bytes 1769480 | tf_op jit(solution)/shard_map/ppermute | solution.py:17
  62.1 42.9 %copy-start.23 = (f32[256]{0:T(256)}, f32[256]{0:T(256)S(1)}, u32[]{:S(2)}) copy-start(f32[256]{0:T(256)S(1)} %broadcast_multiply_fusion.8) | copy-start | bytes 3076
  76.4 26.7 %collective-permute-start.5 = (bf16[384,768]{1,0:T(8,128)(2,1)}, bf16[384,768]{1,0:T(8,128)(2,1)}, u32[]{:S(2)}, u32[]{:S(2)}) collective-permute-start(bf16[384,768]{1,0:T(8,128)(2,1)} %collective-permute-done.4), channel_id=1, source_target_pairs={{0,2},{2,4},{4,6},{6,8},{8,10},{10,12},{12,14},{14,0},{1,3},{3,5},... | collective-permute-start | bytes 1769480 | tf_op jit(solution)/shard_map/ppermute | solution.py:38
  77.6 27.4 %copy-start.27 = (f32[256]{0:T(256)}, f32[256]{0:T(256)S(1)}, u32[]{:S(2)}) copy-start(f32[256]{0:T(256)S(1)} %add_rsqrt_fusion.6) | copy-start | bytes 3076
  103.1 22.9 %collective-permute-start.6 = (bf16[384,768]{1,0:T(8,128)(2,1)}, bf16[384,768]{1,0:T(8,128)(2,1)}, u32[]{:S(2)}, u32[]{:S(2)}) collective-permute-start(bf16[384,768]{1,0:T(8,128)(2,1)} %collective-permute-done.5), channel_id=1, source_target_pairs={{0,2},{2,4},{4,6},{6,8},{8,10},{10,12},{12,14},{14,0},{1,3},{3,5},... | collective-permute-start | bytes 1769480 | tf_op jit(solution)/shard_map/ppermute | solution.py:38
  103.1 1.9 copy-start.12
  105.0 21.0 %copy-start.6 = (bf16[1,256,3072]{2,1,0:T(8,128)(2,1)S(1)}, bf16[1,256,3072]{2,1,0:T(8,128)(2,1)}, u32[]{:S(2)}) copy-start(bf16[1,256,3072]{2,1,0:T(8,128)(2,1)} %param.11) | copy-start | bytes 4718596
  105.0 61.4 %collective-permute-start = (bf16[256,3072]{1,0:T(8,128)(2,1)}, bf16[256,3072]{1,0:T(8,128)(2,1)}, u32[]{:S(2)}, u32[]{:S(2)}) collective-permute-start(bf16[256,3072]{1,0:T(8,128)(2,1)} %fusion.12), channel_id=1, source_target_pairs={{0,1},{1,0},{2,3},{3,2},{4,5},{5,4},{6,7},{7,6},{8,9},{9,8},{10,11... | collective-permute-start | bytes 4718600 | tf_op jit(solution)/shard_map/ppermute | solution.py:17
  106.2 87.3 %collective-permute-start.10 = (bf16[384,768]{1,0:T(8,128)(2,1)}, bf16[384,768]{1,0:T(8,128)(2,1)}, u32[]{:S(2)}, u32[]{:S(2)}) collective-permute-start(bf16[384,768]{1,0:T(8,128)(2,1)} %get-tuple-element.24), channel_id=1, source_target_pairs={{0,1},{1,0},{2,3},{3,2},{4,5},{5,4},{6,7},{7,6},{8,9},{9,8},{10,11... | collective-permute-start | bytes 1769480 | tf_op jit(solution)/shard_map/ppermute | solution.py:17
  126.0 28.8 %collective-permute-start.7 = (bf16[384,768]{1,0:T(8,128)(2,1)}, bf16[384,768]{1,0:T(8,128)(2,1)}, u32[]{:S(2)}, u32[]{:S(2)}) collective-permute-start(bf16[384,768]{1,0:T(8,128)(2,1)} %collective-permute-done.6), channel_id=1, source_target_pairs={{0,2},{2,4},{4,6},{6,8},{8,10},{10,12},{12,14},{14,0},{1,3},{3,5},... | collective-permute-start | bytes 1769480 | tf_op jit(solution)/shard_map/ppermute | solution.py:38
  127.5 59.9 %collective-permute-start.9 = (bf16[256,3072]{1,0:T(8,128)(2,1)}, bf16[256,3072]{1,0:T(8,128)(2,1)}, u32[]{:S(2)}, u32[]{:S(2)}) collective-permute-start(bf16[256,3072]{1,0:T(8,128)(2,1)} %fusion.25), channel_id=1, source_target_pairs={{0,1},{1,0},{2,3},{3,2},{4,5},{5,4},{6,7},{7,6},{8,9},{9,8},{10,11... | collective-permute-start | bytes 4718600 | tf_op jit(solution)/shard_map/ppermute | solution.py:17
  157.0 3.5 %copy-start.5 = (bf16[384,768]{1,0:T(8,128)(2,1)S(1)}, bf16[384,768]{1,0:T(8,128)(2,1)}, u32[]{:S(2)}) copy-start(bf16[384,768]{1,0:T(8,128)(2,1)} %copy-done.4) | copy-start | bytes 1769476
  159.3 1.3 copy-start.3
  166.4 7.0 %copy-start.14 = (bf16[6144,768]{1,0:T(8,128)(2,1)}, bf16[6144,768]{1,0:T(8,128)(2,1)S(1)}, u32[]{:S(2)}) copy-start(bf16[6144,768]{1,0:T(8,128)(2,1)S(1)} %constant_dynamic-update-slice_fusion) | copy-start | bytes 28311556
  173.4 11.7 %copy-start.1 = (f32[512,768]{1,0:T(8,128)}, f32[512,768]{1,0:T(8,128)S(1)}, u32[]{:S(2)}) copy-start(f32[512,768]{1,0:T(8,128)S(1)} %fusion.3) | copy-start | bytes 4718596
  173.4 0.7 copy-start.25
  173.9 2.4 %copy-start.21 = (f32[512]{0:T(512)}, f32[512]{0:T(512)S(1)}, u32[]{:S(2)}) copy-start(f32[512]{0:T(512)S(1)} %get-tuple-element.57) | copy-start | bytes 6148
  173.9 9.0 %copy-start.15 = (f32[512]{0:T(512)}, f32[512]{0:T(512)S(1)}, u32[]{:S(2)}) copy-start(f32[512]{0:T(512)S(1)} %get-tuple-element.56) | copy-start | bytes 6148
  173.9 11.2 %copy-start.29 = (f32[512]{0:T(512)}, f32[512]{0:T(512)S(1)}, u32[]{:S(2)}) copy-start(f32[512]{0:T(512)S(1)} %get-tuple-element.52) | copy-start | bytes 6148
  176.3 4.4 %copy-start.17 = (f32[512]{0:T(512)}, f32[512]{0:T(512)S(1)}, u32[]{:S(2)}) copy-start(f32[512]{0:T(512)S(1)} %get-tuple-element.54) | copy-start | bytes 6148
  176.3 4.4 %copy-start.19 = (f32[512]{0:T(512)}, f32[512]{0:T(512)S(1)}, u32[]{:S(2)}) copy-start(f32[512]{0:T(512)S(1)} %get-tuple-element.55) | copy-start | bytes 6148
  187.4 6.1 %copy-start.13 = (bf16[384,768]{1,0:T(8,128)(2,1)S(1)}, bf16[384,768]{1,0:T(8,128)(2,1)}, u32[]{:S(2)}) copy-start(bf16[384,768]{1,0:T(8,128)(2,1)} %get-tuple-element.25) | copy-start | bytes 1769476
  187.4 6.1 %copy-start.11 = (f32[512,768]{1,0:T(8,128)S(1)}, f32[512,768]{1,0:T(8,128)}, u32[]{:S(2)}) copy-start(f32[512,768]{1,0:T(8,128)} %get-tuple-element.27) | copy-start | bytes 4718596
  193.5 1.4 copy-start.26
  193.5 1.4 copy-start.35
  194.9 1.4 copy-start.10
  194.9 1.4 copy-start.34
  197.7 1.4 copy-start.9
  197.7 1.4 copy-start.33
  200.4 1.4 copy-start.8
  200.5 1.4 copy-start.32
  203.2 1.4 copy-start.7
  203.2 1.4 copy-start.31
  206.0 1.4 copy-start.36
  206.0 1.4 copy-start.37
  206.0 2.9 %copy-start.16 = (f32[512]{0:T(512)S(1)}, f32[512]{0:T(512)}, u32[]{:S(2)}) copy-start(f32[512]{0:T(512)} %copy-done.15) | copy-start | bytes 6148
  206.0 2.9 %copy-start.18 = (f32[512]{0:T(512)S(1)}, f32[512]{0:T(512)}, u32[]{:S(2)}) copy-start(f32[512]{0:T(512)} %copy-done.17) | copy-start | bytes 6148
  206.0 2.9 %copy-start.20 = (f32[512]{0:T(512)S(1)}, f32[512]{0:T(512)}, u32[]{:S(2)}) copy-start(f32[512]{0:T(512)} %copy-done.19) | copy-start | bytes 6148
  206.0 2.9 %copy-start.22 = (f32[512]{0:T(512)S(1)}, f32[512]{0:T(512)}, u32[]{:S(2)}) copy-start(f32[512]{0:T(512)} %copy-done.21) | copy-start | bytes 6148
  206.0 2.9 %copy-start.30 = (f32[512]{0:T(512)S(1)}, f32[512]{0:T(512)}, u32[]{:S(2)}) copy-start(f32[512]{0:T(512)} %copy-done.29) | copy-start | bytes 6148
  207.4 1.6 copy-start.2
  207.4 4.3 %slice-start = ((s8[9437184]{0:T(1024)(128)(4,1)}), s8[4194304]{0:T(1024)(128)(4,1)S(1)}, s32[]{:S(2)}) async-start(s8[9437184]{0:T(1024)(128)(4,1)} %bitcast.59), calls=%async_computation.1 | async-start | bytes 8388608
  207.4 4.3 %slice-start.1 = ((s8[9437184]{0:T(1024)(128)(4,1)}), s8[4194304]{0:T(1024)(128)(4,1)S(1)}, s32[]{:S(2)}) async-start(s8[9437184]{0:T(1024)(128)(4,1)} %bitcast.59), calls=%async_computation.2 | async-start | bytes 8388608
  209.0 2.8 %slice-start.2 = ((s8[9437184]{0:T(1024)(128)(4,1)}), s8[1048576]{0:T(1024)(128)(4,1)S(1)}, s32[]{:S(2)}) async-start(s8[9437184]{0:T(1024)(128)(4,1)} %bitcast.59), calls=%async_computation.3 | async-start | bytes 2097152
  211.8 4.9 %copy-start.24 = (f32[256]{0:T(256)S(1)}, f32[256]{0:T(256)}, u32[]{:S(2)}) copy-start(f32[256]{0:T(256)} %copy-done.23) | copy-start | bytes 3076
  211.8 4.9 %copy-start.28 = (f32[256]{0:T(256)S(1)}, f32[256]{0:T(256)}, u32[]{:S(2)}) copy-start(f32[256]{0:T(256)} %copy-done.27) | copy-start | bytes 3076
  213.3 3.5 %collective-permute-start.11 = (bf16[256,3072]{1,0:T(8,128)(2,1)S(1)}, bf16[256,3072]{1,0:T(8,128)(2,1)S(1)}, u32[]{:S(2)}, u32[]{:S(2)}) collective-permute-start(bf16[256,3072]{1,0:T(8,128)(2,1)S(1)} %convolution_convert_fusion), channel_id=1, source_target_pairs={{0,1},{1,0},{2,3},{3,2},{4,5},{5,4},{6,7},{7,6},{8,9},{9,8},{10,11... | collective-permute-start | bytes 4718600 | tf_op jit(solution)/shard_map/ppermute | solution.py:17
Sparse Core Ops, SparseCore 0:
  59.8 111.3 all-gather.1
